TPU v7x, 32 devices: a whole 2x2x4 slice. The times are simulated.
32 devices in a mesh: section: 2 (over core), group: 4 (over y, x), tensor: 4 (over z).
Axes of the slice: x: 2, y: 2, z: 4, core: 2. Of those that a mesh axis runs over, the one named last changes fastest.
Arguments:
- queries: bfloat16 [64, 3072], P(('section', 'group'), 'tensor'), may hold values from -140 to 140
- new_kv: bfloat16 [64, 2048], P(('section', 'group'), 'tensor'), may hold values from -10 to 10
- kv_cache: bfloat16 [8, 2048, 2048], P(('section', 'group'), None, 'tensor'), may hold values from -4.5 to 4.5
- cache_len: int32 [8], P(('section', 'group')), may hold values from 1 to 2048, 10240 in all
- residual: bfloat16 [64, 3072], P(('section', 'group'), 'tensor'), may hold values from -28 to 28
- norm_gain: bfloat16 [3072], P('tensor'), may hold values from 0.099609375 to 1.8984375
- router: bfloat16 [8, 3072], P(None, 'tensor'), may hold values from -0.23925781 to 0.23925781
- routes: int32 [64, 4], P(('section', 'group')), may hold values from 0 to 7, all different within a row; in each aligned block of 8 rows (0 to 7, 8 to 15, ...) at most 8 rows name the same one
- gate_w: bfloat16 [8, 6912, 3072], P(('section', 'tensor'), 'group'), may hold values from -0.109375 to 0.109375
- up_w: bfloat16 [8, 6912, 3072], P(('section', 'tensor'), 'group'), may hold values from -0.109375 to 0.109375
- down_w: bfloat16 [8, 6912, 3072], P(('section', 'tensor'), 'group'), may hold values from -0.078125 to 0.078125
Outputs:
- mixed: bfloat16 [64, 3072], P(('section', 'group'), 'tensor')
Inputs may be any that keep to these rules, and one draw needn't show every extreme that they name: `routes`: each token names 4 different experts; in each aligned block of 8 tokens (the branches of one prefix) no expert is named by more than 8 tokens, and in some block one expert is named by exactly 8. `cache_len`: the largest is 2048.
All inputs are finite; a program needn't handle non-finite values. No bound on the sum of `cache_len` on one device may be relied on, other than what follows from the above.
Results may differ from a plain program's by a relative error of at most 0.0065.
Values may be sent and summed in bfloat16 or wider, within the bound.
No kernel may reach another device: no remote copies, remote signals or barrier semaphores. Data moves between devices by JAX's collectives and lax.ppermute only.
A program may use at most 128 MiB of HBM per device.

v0:
```python
import jax
import jax.numpy as jnp
from jax import lax
from jax.sharding import PartitionSpec as P

D = 3072
HEAD_DIM = 128


norm_eps = 1e-05


def key_views(queries, new_kv, kv_cache):
    tokens = queries.shape[0]
    key_heads = new_kv.shape[1] // (2 * HEAD_DIM)
    grouped = queries.shape[1] // HEAD_DIM // key_heads
    query_head_rows = queries.reshape(tokens, key_heads, grouped, HEAD_DIM)
    latest_token_view = new_kv.reshape(tokens, key_heads, 2, HEAD_DIM)
    cache_view = kv_cache.reshape(-1, key_heads, 2, HEAD_DIM)
    return (query_head_rows, latest_token_view, cache_view)


def block_scores(query_head_rows, cached_key_rows):
    return jnp.einsum(
        "tkgd,jkd->tkgj", query_head_rows, cached_key_rows, preferred_element_type=jnp.float32
    ) * HEAD_DIM ** (-0.5)


def attend_whole_cache(query_head_rows, cache_view, length, self_token_score):
    positions = jnp.arange(cache_view.shape[0])
    scores = jnp.where(
        positions < length, block_scores(query_head_rows, cache_view[:, :, 0]), -jnp.inf
    )
    row_max = jnp.maximum(jnp.max(scores, -1), self_token_score)
    weights = jnp.exp(scores - row_max[..., None]).astype(jnp.bfloat16)
    numerator = jnp.einsum(
        "tkgj,jkd->tkgd", weights, cache_view[:, :, 1], preferred_element_type=jnp.float32
    )
    softmax_divisor = jnp.sum(weights, -1, dtype=jnp.float32)
    return (row_max, numerator, softmax_divisor)


def normalize(stream_float, total_sum, square_sum, gain):
    mean_value = total_sum / D
    variance = square_sum / D - mean_value * mean_value
    inv_std = lax.rsqrt(variance + norm_eps)
    return (
        (stream_float - mean_value[:, None]) * inv_std[:, None] * gain.astype(jnp.float32)
    ).astype(jnp.bfloat16)


def routing_tables(routes, logits, experts, capacity):
    tokens, choose = routes.shape
    flat_routes = routes.reshape(-1)
    onehot_rows = (flat_routes[:, None] == jnp.arange(experts)[None, :]).astype(jnp.int32)
    earlier = jnp.cumsum(onehot_rows, 0) - onehot_rows
    slot_index = jnp.sum(earlier * onehot_rows, 1)
    destination = flat_routes * capacity + slot_index
    placed = (destination[:, None] == jnp.arange(experts * capacity)[None, :]).reshape(
        tokens, choose, experts * capacity
    )
    picked = jnp.sum(
        jnp.where(onehot_rows.reshape(tokens, choose, experts) > 0, logits[:, None, :], 0.0), -1
    )
    raised = jnp.exp(picked)
    gate_share = raised / jnp.sum(raised, -1, keepdims=True)
    selector = jnp.transpose(jnp.any(placed, 1)).astype(jnp.bfloat16)
    combine = jnp.sum(jnp.where(placed, gate_share[:, :, None], 0.0), 1)
    return (selector, combine)


def per_device(
    queries, new_kv, kv_cache, cache_len, residual, norm_gain, router, routes, gate_w, up_w, down_w
):
    sections = lax.axis_size("section")
    groups = lax.axis_size("group")
    tensors = lax.axis_size("tensor")
    experts = sections * tensors
    tokens = queries.shape[0]
    capacity = max(2, min(tokens, 2 * tokens * routes.shape[1] // experts))
    model_width = D
    query_head_rows, latest_token_view, cache_view = key_views(queries, new_kv, kv_cache)
    self_token_score = jnp.einsum(
        "tkgd,tkd->tkg",
        query_head_rows,
        latest_token_view[:, :, 0],
        preferred_element_type=jnp.float32,
    ) * HEAD_DIM ** (-0.5)
    row_max, numerator, softmax_divisor = attend_whole_cache(
        query_head_rows, cache_view, cache_len[0], self_token_score
    )
    own_weight = jnp.exp(self_token_score - row_max).astype(jnp.bfloat16).astype(jnp.float32)
    numerator = numerator + own_weight[..., None] * latest_token_view[:, :, 1][
        :, :, None, :
    ].astype(jnp.float32)
    softmax_divisor = softmax_divisor + own_weight
    attention = (numerator / softmax_divisor[..., None]).reshape(tokens, -1)
    stream = (residual.astype(jnp.float32) + attention).astype(jnp.bfloat16)
    stream_all, gain_all, router_all = (
        lax.all_gather(stream, "tensor", axis=1, tiled=True),
        lax.all_gather(norm_gain, "tensor", axis=0, tiled=True),
        lax.all_gather(router, "tensor", axis=1, tiled=True),
    )
    stream_float = stream_all.astype(jnp.float32)
    normed = normalize(
        stream_float, jnp.sum(stream_float, 1), jnp.sum(stream_float * stream_float, 1), gain_all
    )
    logits = lax.dot_general(
        normed, router_all, (((1,), (1,)), ((), ())), preferred_element_type=jnp.float32
    )
    selector, combine = routing_tables(routes, logits, experts, capacity)
    own_rows = lax.dynamic_index_in_dim(
        selector.reshape(sections, tensors, capacity, tokens),
        lax.axis_index("tensor"),
        1,
        keepdims=False,
    )
    arrived = jnp.dot(
        own_rows.reshape(-1, tokens), normed, preferred_element_type=jnp.float32
    ).astype(jnp.bfloat16)
    arrived = arrived.reshape(sections, capacity, model_width)
    gate_local = gate_w[0]
    up_local = up_w[0]
    down_local = down_w[0]
    spread_rows = jnp.broadcast_to(
        arrived[:, None], (sections, groups, capacity, model_width)
    ).reshape(sections * groups, capacity, model_width)
    received = lax.all_to_all(
        spread_rows, ("section", "group"), split_axis=0, concat_axis=0, tiled=True
    )
    flat_rows = received.reshape(-1, model_width)
    gate_part = lax.dot_general(
        flat_rows, gate_local, (((1,), (1,)), ((), ())), preferred_element_type=jnp.float32
    )
    up_part = lax.dot_general(
        flat_rows, up_local, (((1,), (1,)), ((), ())), preferred_element_type=jnp.float32
    )
    hidden = (jax.nn.silu(gate_part) * up_part).astype(jnp.bfloat16)
    hidden = (
        hidden.reshape(sections, groups, capacity, -1)
        .transpose(1, 0, 2, 3)
        .reshape(groups * sections * capacity, -1)
    )
    summed = lax.psum_scatter(
        jnp.dot(hidden, down_local, preferred_element_type=jnp.float32).astype(jnp.bfloat16),
        "group",
        scatter_dimension=0,
        tiled=True,
    )
    returned = lax.all_to_all(
        lax.all_to_all(
            summed.reshape(sections, capacity, model_width),
            "section",
            split_axis=0,
            concat_axis=0,
            tiled=True,
        ),
        "tensor",
        split_axis=2,
        concat_axis=0,
        tiled=True,
    )
    returned = (
        returned.reshape(tensors, sections, capacity, -1)
        .transpose(1, 0, 2, 3)
        .reshape(experts * capacity, -1)
    )
    expert_mix = jnp.dot(combine, returned.astype(jnp.float32), precision=lax.Precision.HIGHEST)
    return (stream.astype(jnp.float32) + expert_mix).astype(jnp.bfloat16)


def solution(mesh):
    in_specs = (
        P(("section", "group"), "tensor"),
        P(("section", "group"), "tensor"),
        P(("section", "group"), None, "tensor"),
        P(("section", "group")),
        P(("section", "group"), "tensor"),
        P("tensor"),
        P(None, "tensor"),
        P(("section", "group"), None),
        P(("section", "tensor"), "group", None),
        P(("section", "tensor"), "group", None),
        P(("section", "tensor"), "group", None),
    )
    out_specs = P(("section", "group"), "tensor")
    return jax.shard_map(
        per_device, mesh=mesh, in_specs=in_specs, out_specs=out_specs, check_vma=False
    )
```

profile of v0, /device:TPU:0, one launch (start us, length us, event | category | flops | bytes accessed | tf_op | source)
XLA Modules:
  0.0 124.2 jit_solution(9106268146351577279)
XLA Ops:
  6.5 2.9 %copy.69 = bf16[1,2048,512]{1,2,0:T(8,128)(2,1)S(1)} copy(bf16[1,2048,512]{2,1,0:T(8,128)(2,1)} %param.13) | data formatting | bytes 4194304 | tf_op args[2]
  10.1 0.7 fusion.33
  10.8 0.8 fusion.29
  11.7 0.1 copy.84
  11.8 1.1 fusion.41
  12.8 0.2 convert_reduce_fusion
  13.1 0.4 fusion.19
  13.5 0.7 add_convert_fusion
  14.2 14.7 %all_gather.9 = bf16[8,3072]{1,0:T(8,128)(2,1)S(1)} all-gather(bf16[8,768]{1,0:T(8,128)(2,1)S(1)} %add_convert_fusion), channel_id=1, replica_groups=mesh['section'=2,'group'=4,'tensor'=4] {'tensor'}, dimensions={1}, use_global_device_ids=true | all-gather | bytes 61440 | tf_op jit(solution)/shard_map/all_gather | solution.py:100
  29.0 0.2 convert_reduce_fusion.1
  29.1 0.8 copy.73
  30.1 0.2 select_reduce_fusion.2
  30.5 0.1 reshape.108
  30.8 0.8 reshape.117
  31.6 13.2 %all-gather = bf16[4,1,768]{2,1,0:T(2,128)(2,1)S(1)} all-gather(bf16[1,1,768]{2,1,0:T(2,128)(2,1)S(1)} %reshape.117), channel_id=1, replica_groups=mesh['section'=2,'group'=4,'tensor'=4] {'tensor'}, dimensions={0}, use_global_device_ids=true | all-gather | bytes 7680 | tf_op jit(solution)/shard_map/all_gather | solution.py:101
  44.8 0.2 fusion.9
  45.1 11.7 %all_to_all.22 = bf16[8,8,3072]{2,1,0:T(8,128)(2,1)S(1)} all-to-all(bf16[8,8,3072]{2,1,0:T(8,128)(2,1)S(1)} %bitcast.102), channel_id=1, replica_groups=mesh['section'=2,'group'=4,'tensor'=4] {'section','group'}, dimensions={0} | all-to-all | bytes 786432 | tf_op jit(solution)/shard_map/all_to_all | solution.py:128
  56.7 7.5 %fusion.4 = f32[64,1728]{1,0:T(8,128)S(1)} fusion(bf16[1,1728,3072]{2,1,0:T(8,128)(2,1)} %param.19, bf16[8,8,3072]{2,1,0:T(8,128)(2,1)S(1)} %all_to_all.22), kind=kOutput, calls=%fused_computation.4 | convolution fusion | flops 679477248 | bytes 11452416 | tf_op jit(solution)/shard_map/dot_general | solution.py:132
  64.2 3.3 %fusion.13 = bf16[64,1728]{1,0:T(8,128)(2,1)S(1)} fusion(bf16[1,1728,3072]{2,1,0:T(8,128)(2,1)S(1)} %copy-done, f32[64,1728]{1,0:T(8,128)S(1)} %fusion.4, bf16[8,8,3072]{2,1,0:T(8,128)(2,1)S(1)} %all_to_all.22), kind=kOutput, calls=%fused_computation.10 | convolution fusion | flops 680140800 | bytes 11673600 | tf_op jit(solution)/shard_map/dot_general | solution.py:135
  67.7 2.8 %fusion.6 = bf16[64,3072]{1,0:T(8,128)(2,1)} fusion(bf16[64,1728]{1,0:T(8,128)(2,1)S(1)} %bitcast.103, bf16[1,1728,3072]{2,1,0:T(8,128)(2,1)S(1)} %bitcast.97), kind=kOutput, calls=%fused_computation.6 | convolution fusion | flops 679673856 | bytes 11231232 | tf_op jit(solution)/shard_map/dot_general | solution.py:145
  70.5 13.1 %all_gather.11 = bf16[8,3072]{1,0:T(8,128)(2,1)S(1)} all-gather(bf16[8,768]{1,0:T(8,128)(2,1)S(1)} %copy-done.1), channel_id=1, replica_groups=mesh['section'=2,'group'=4,'tensor'=4] {'tensor'}, dimensions={1}, use_global_device_ids=true | all-gather | bytes 61440 | tf_op jit(solution)/shard_map/all_gather | solution.py:102
  83.5 0.2 fusion.37
  83.7 0.2 select_reduce_fusion.1
  83.9 10.5 %reduce-scatter.2.cloned.1.call-done = bf16[16,3072]{1,0:T(8,128)(2,1)} async-done(((bf16[64,3072]{1,0:T(8,128)(2,1)}), bf16[16,3072]{1,0:T(8,128)(2,1)}) %reduce-scatter.2.cloned.1.call-update) | async-done | bytes 98320 | tf_op jit(solution)/shard_map/reduce_scatter | solution.py:144
  94.4 4.8 %all_to_all.23 = bf16[2,8,3072]{2,1,0:T(8,128)(2,1)S(1)} all-to-all(bf16[2,8,3072]{2,1,0:T(8,128)(2,1)} %bitcast.107), channel_id=1, replica_groups=mesh['section'=2,'group'=4,'tensor'=4] {'section'}, dimensions={0} | all-to-all | bytes 196608 | tf_op jit(solution)/shard_map/all_to_all | solution.py:151
  99.2 1.8 %copy.78 = bf16[2,8,3072]{1,0,2:T(2,128)(2,1)S(1)} copy(bf16[2,8,3072]{2,1,0:T(8,128)(2,1)S(1)} %all_to_all.23) | data formatting | bytes 196608 | tf_op jit(solution)/shard_map/all_to_all | solution.py:151
  101.0 2.3 %reshape.124 = bf16[4,2,6144]{2,1,0:T(2,128)(2,1)} reshape(bf16[3072,2,8]{2,1,0:T(2,128)(2,1)S(1)} %bitcast.98) | data formatting | bytes 196608
  103.2 4.6 %all-to-all-start.2 = ((bf16[4,2,6144]{2,1,0:T(2,128)(2,1)}), bf16[4,2,6144]{2,1,0:T(2,128)(2,1)S(1)}, u32[]{:S(2)}, u32[]{:S(2)}) async-start(bf16[4,2,6144]{2,1,0:T(2,128)(2,1)} %reshape.124), calls=%async_computation.3 | async-start | bytes 196608 | tf_op jit(solution)/shard_map/all_to_all | solution.py:150
  107.9 5.7 %all-to-all-done.2 = bf16[4,2,6144]{2,1,0:T(2,128)(2,1)S(1)} async-done(((bf16[4,2,6144]{2,1,0:T(2,128)(2,1)}), bf16[4,2,6144]{2,1,0:T(2,128)(2,1)S(1)}, u32[]{:S(2)}, u32[]{:S(2)}) %all-to-all-start.2) | async-done | bytes 98336 | tf_op jit(solution)/shard_map/all_to_all | solution.py:150
  113.7 1.8 %reshape.125 = bf16[3072,2,8]{2,1,0:T(2,128)(2,1)S(1)} reshape(bf16[4,2,6144]{2,1,0:T(2,128)(2,1)S(1)} %all-to-all-done.2) | data formatting | bytes 196608
  115.5 1.0 copy.86
  116.6 0.8 fusion.20
  (35 shorter events, 0.8 us)
Async XLA Ops:
  6.5 87.9 %reduce-scatter.2.cloned.1.call-start = ((), (), s32[]{:S(2)}) async-start(), calls=%async_computation.4 | async-start | bytes 491520 | tf_op jit(solution)/shard_map/reduce_scatter | solution.py:144
  30.8 33.5 %copy-start = (bf16[1,1728,3072]{2,1,0:T(8,128)(2,1)S(1)}, bf16[1,1728,3072]{2,1,0:T(8,128)(2,1)}, u32[]{:S(2)}) copy-start(bf16[1,1728,3072]{2,1,0:T(8,128)(2,1)} %param.20) | copy-start | bytes 31850500
  56.7 10.9 %slice-start = ((s8[10616832]{0:T(1024)(128)(4,1)}), s8[4194304]{0:T(1024)(128)(4,1)S(1)}, s32[]{:S(2)}) async-start(s8[10616832]{0:T(1024)(128)(4,1)} %bitcast.96), calls=%async_computation.5 | async-start | bytes 8388608
  56.7 10.9 %slice-start.1 = ((s8[10616832]{0:T(1024)(128)(4,1)}), s8[4194304]{0:T(1024)(128)(4,1)S(1)}, s32[]{:S(2)}) async-start(s8[10616832]{0:T(1024)(128)(4,1)} %bitcast.96), calls=%async_computation.6 | async-start | bytes 8388608
  64.2 3.4 %slice-start.2 = ((s8[10616832]{0:T(1024)(128)(4,1)}), s8[2228224]{0:T(1024)(128)(4,1)S(1)}, s32[]{:S(2)}) async-start(s8[10616832]{0:T(1024)(128)(4,1)} %bitcast.96), calls=%async_computation.7 | async-start | bytes 4456448
  67.6 2.9 %copy-start.1 = (bf16[8,768]{1,0:T(8,128)(2,1)S(1)}, bf16[8,768]{1,0:T(8,128)(2,1)}, u32[]{:S(2)}) copy-start(bf16[8,768]{1,0:T(8,128)(2,1)} %param.17) | copy-start | bytes 36868
  67.6 16.2 %copy-start.2 = (s32[8,4]{0,1:T(4,128)S(1)}, s32[8,4]{0,1:T(4,128)}, u32[]{:S(2)}) copy-start(s32[8,4]{0,1:T(4,128)} %param.18) | copy-start | bytes 388
  103.2 10.4 %all-to-all-start.2 = ((bf16[4,2,6144]{2,1,0:T(2,128)(2,1)}), bf16[4,2,6144]{2,1,0:T(2,128)(2,1)S(1)}, u32[]{:S(2)}, u32[]{:S(2)}) async-start(bf16[4,2,6144]{2,1,0:T(2,128)(2,1)} %reshape.124), calls=%async_computation.3 | async-start | bytes 196608 | tf_op jit(solution)/shard_map/all_to_all | solution.py:150
Sparse Core Ops, SparseCore 0:
  70.6 23.7 reduce-scatter.1
where the time goes:
time: 125 us; the launch traced here: 124 us
  blocking collectives  57.4 us (46%)
  matrix products  17.1 us (14%)
  waiting for transfers between devices  16.2 us (13%)
  between operations  14.2 us (11%)
  local copies, waits for them, and re-layouts  12.1 us (10%)
  starting transfers between devices  4.61 us (4%)
  other arithmetic  2.53 us (2%)
    all_gather x1, blocking collectives, per_device(): lax.all_gather(stream, 'tensor', axis=1, tiled=True)  14.7 us
    all_gather x1, blocking collectives, per_device(): lax.all_gather(norm_gain, 'tensor', axis=0, tiled=True)  13.2 us
    all_gather x1, blocking collectives, per_device(): lax.all_gather(router, 'tensor', axis=1, tiled=True)  13.1 us
    all_to_all x1, blocking collectives, per_device(): lax.all_to_all(spread_rows, ('section', 'group'), split_axis=0, concat_ax...  11.7 us
    reduce_scatter x1, waiting for transfers between devices, per_device(): lax.psum_scatter(jnp.dot(hidden, down_local, preferred_element_type=jnp.f...  10.5 us
    unnamed x17, local copies, waits for them, and re-layouts  8.66 us
    dot_general x1, matrix products, per_device(): lax.dot_general(flat_rows, gate_local, (((1,), (1,)), ((), ())), preferre...  7.47 us
    all_to_all x1, waiting for transfers between devices, per_device(): lax.all_to_all(lax.all_to_all(summed.reshape(sections, capacity, model_wi...  5.75 us
  transfers between devices with their start and end apart: 2, of which 2 were waited for; matrix products, arithmetic and copies ran while one was open for 0% of the time, Pallas kernels for 0%

commit v1 on v0

v1 whole, which is shorter than its diff:
```python
import functools

import jax
import jax.numpy as jnp
from jax import lax
from jax.experimental import pallas as pl
from jax.experimental.pallas import tpu as pltpu
from jax.sharding import PartitionSpec as P

HEAD_DIM = 128
NORM_EPS = 1e-05
LANES = 128
MIB = 1 << 20


def attention_kernel(len_ref, q_ref, new_ref, kv_hbm, res_ref, routes_ref, out_ref, kv, scores, sems, *, chunks):
    slots = kv_hbm.shape[1]
    part = slots // chunks
    copies = []
    for c in range(chunks):
        rows = pl.ds(c * part, part)
        copies.append(pltpu.make_async_copy(kv_hbm.at[0, rows], kv.at[rows], sems.at[c]))
        copies[-1].start()
    tokens, columns = q_ref.shape
    key_heads = new_ref.shape[1] // (2 * HEAD_DIM)
    grouped = columns // HEAD_DIM // key_heads
    rows = grouped * tokens
    scale = HEAD_DIM ** (-0.5)
    queries, selves = [], []
    for h in range(key_heads):
        first = h * grouped * HEAD_DIM
        q = jnp.concatenate(
            [
                q_ref[:, first + j * HEAD_DIM : first + (j + 1) * HEAD_DIM].astype(jnp.float32)
                for j in range(grouped)
            ],
            axis=0,
        )
        own_key = new_ref[:, 2 * h * HEAD_DIM : (2 * h + 1) * HEAD_DIM].astype(jnp.float32)
        own_key = jnp.concatenate([own_key] * grouped, axis=0)
        selves.append(jnp.sum(q * own_key, axis=1, keepdims=True) * scale)
        queries.append(q.astype(jnp.bfloat16))
    experts = LANES
    routes = routes_ref[...]
    expert_at = lax.broadcasted_iota(jnp.int32, (experts, tokens), 0)
    named = jnp.zeros((experts, tokens), jnp.float32)
    for k in range(routes.shape[0]):
        named = jnp.where(expert_at == routes[k : k + 1, :], 1.0, named)
    out_ref[:, columns:] = named.T.astype(out_ref.dtype)
    live = len_ref[0]
    for c in range(chunks):
        copies[c].wait()
        for h in range(key_heads):
            keys = kv[c * part : (c + 1) * part, 2 * h * HEAD_DIM : (2 * h + 1) * HEAD_DIM]
            s = lax.dot_general(
                queries[h], keys, (((1,), (1,)), ((), ())), preferred_element_type=jnp.float32
            )
            at = lax.broadcasted_iota(jnp.int32, (rows, part), 1) + c * part
            scores[h, :, c * part : (c + 1) * part] = jnp.where(at < live, s * scale, -jnp.inf)
    for h in range(key_heads):
        s = scores[h]
        top = jnp.maximum(jnp.max(s, axis=1, keepdims=True), selves[h])
        weights = jnp.exp(s - top).astype(jnp.bfloat16)
        own = jnp.exp(selves[h] - top).astype(jnp.bfloat16).astype(jnp.float32)
        total = jnp.sum(weights.astype(jnp.float32), axis=1, keepdims=True) + own
        value_at = (2 * h + 1) * HEAD_DIM
        mixed = jnp.dot(weights, kv[:, value_at : value_at + HEAD_DIM], preferred_element_type=jnp.float32)
        own_value = new_ref[:, value_at : value_at + HEAD_DIM].astype(jnp.float32)
        mixed = (mixed + own * jnp.concatenate([own_value] * grouped, axis=0)) / total
        for j in range(grouped):
            at = (h * grouped + j) * HEAD_DIM
            got = res_ref[:, at : at + HEAD_DIM].astype(jnp.float32) + mixed[j * tokens : (j + 1) * tokens]
            out_ref[:, at : at + HEAD_DIM] = got.astype(out_ref.dtype)


def attend(cache_len, queries, new_kv, kv_cache, residual, routes):
    tokens, columns = queries.shape
    slots, width = kv_cache.shape[1:]
    key_heads = new_kv.shape[1] // (2 * HEAD_DIM)
    rows = columns // HEAD_DIM // key_heads * tokens
    chunks = 4
    vmem = pl.BlockSpec(memory_space=pltpu.VMEM)
    return pl.pallas_call(
        functools.partial(attention_kernel, chunks=chunks),
        out_shape=jax.ShapeDtypeStruct((tokens, columns + LANES), jnp.bfloat16),
        in_specs=[
            pl.BlockSpec(memory_space=pltpu.SMEM),
            vmem,
            vmem,
            pl.BlockSpec(memory_space=pl.ANY),
            vmem,
            vmem,
        ],
        out_specs=vmem,
        scratch_shapes=[
            pltpu.VMEM((slots, width), kv_cache.dtype),
            pltpu.VMEM((key_heads, rows, slots), jnp.float32),
            pltpu.SemaphoreType.DMA((chunks,)),
        ],
        compiler_params=pltpu.CompilerParams(vmem_limit_bytes=8 * MIB),
        cost_estimate=pl.CostEstimate(
            flops=4 * rows * slots * HEAD_DIM * key_heads,
            bytes_accessed=slots * width * 2,
            transcendentals=rows * slots * key_heads,
        ),
        name="attention",
    )(cache_len, queries, new_kv, kv_cache, residual, routes.T)


def expert_kernel(place_ref, near_ref, far_ref, *refs, ranks, tensors, experts):
    params = refs[:tensors]
    gate_ref, up_ref, down_ref, near_out, far_out, normed, hidden, share = refs[tensors:]
    place, expert = place_ref[0], place_ref[1]
    tokens, block = near_ref.shape[2], near_out.shape[3]
    model = tensors * block
    half = ranks * tokens

    def column(k):
        return pl.multiple_of(lax.rem(place - k + tensors, tensors) * block, block)

    pair = 2
    for side, ref in enumerate((near_ref, far_ref)):
        for g in range(0, ranks, pair):
            pieces = [
                jnp.concatenate(
                    [ref[g + p, k, :, :block].astype(jnp.float32) for p in range(pair)], axis=0
                )
                for k in range(tensors)
            ]
            mean = sum(jnp.sum(x, axis=1, keepdims=True) for x in pieces) / model
            square = sum(jnp.sum(x * x, axis=1, keepdims=True) for x in pieces) / model
            inv = lax.rsqrt(square - mean * mean + NORM_EPS)
            at = side * half + g * tokens
            logits = jnp.zeros((pair * tokens, experts), jnp.float32)
            for k in range(tensors):
                gain = params[k][experts : experts + 1, :].astype(jnp.float32)
                x = ((pieces[k] - mean) * inv * gain).astype(jnp.bfloat16)
                normed[at : at + pair * tokens, pl.ds(column(k), block)] = x
                logits += lax.dot_general(
                    x, params[k][:experts, :], (((1,), (1,)), ((), ())), preferred_element_type=jnp.float32
                )
            named = jnp.concatenate(
                [ref[g + p, 0, :, block:].astype(jnp.float32)[:, :experts] for p in range(pair)], axis=0
            )
            raised = jnp.where(named > 0, jnp.exp(logits), 0.0)
            lane = lax.broadcasted_iota(jnp.int32, raised.shape, 1)
            mine = jnp.sum(jnp.where(lane == expert, raised, 0.0), axis=1, keepdims=True)
            share[at : at + pair * tokens, :] = jnp.broadcast_to(
                mine / jnp.sum(raised, axis=1, keepdims=True), (pair * tokens, LANES)
            )

    units = gate_ref.shape[1]
    step = 256

    def up_block(at, size):
        x = normed[...]
        contract = (((1,), (1,)), ((), ()))
        a = lax.dot_general(x, gate_ref[0, pl.ds(at, size), :], contract, preferred_element_type=jnp.float32)
        b = lax.dot_general(x, up_ref[0, pl.ds(at, size), :], contract, preferred_element_type=jnp.float32)
        hidden[:, pl.ds(at, size)] = (a / (1.0 + jnp.exp(-a)) * b).astype(jnp.bfloat16)

    @pl.loop(0, units // step)
    def _(i):
        up_block(pl.multiple_of(i * step, step), step)

    if units % step:
        up_block(units // step * step, units % step)

    for k in range(tensors):
        part = jnp.dot(hidden[...], down_ref[0, :, pl.ds(column(k), block)], preferred_element_type=jnp.float32)
        part = part * share[:, :1]
        for side, ref in enumerate((near_out, far_out)):
            for g in range(ranks):
                at = side * half + g * tokens
                ref[g, k] = part[at : at + tokens].astype(ref.dtype)


def run_expert(place, near, far, params, gate_w, up_w, down_w, experts):
    ranks, tensors, tokens, wide = near.shape
    block = wide - LANES
    units, model = gate_w.shape[1:]
    rows = 2 * ranks * tokens
    vmem = pl.BlockSpec(memory_space=pltpu.VMEM)
    weight = pl.BlockSpec(memory_space=pltpu.VMEM)
    shape = jax.ShapeDtypeStruct((ranks, tensors, tokens, block), jnp.bfloat16)
    weights = [pltpu.with_memory_space_constraint(w, pltpu.VMEM) for w in (gate_w, up_w, down_w)]
    return pl.pallas_call(
        functools.partial(expert_kernel, ranks=ranks, tensors=tensors, experts=experts),
        out_shape=(shape, shape),
        in_specs=[pl.BlockSpec(memory_space=pltpu.SMEM), vmem, vmem] + [vmem] * tensors + [weight] * 3,
        out_specs=(vmem, vmem),
        scratch_shapes=[
            pltpu.VMEM((rows, model), jnp.bfloat16),
            pltpu.VMEM((rows, units), jnp.bfloat16),
            pltpu.VMEM((rows, LANES), jnp.float32),
        ],
        compiler_params=pltpu.CompilerParams(vmem_limit_bytes=(10 if rows <= 64 else 24) * MIB),
        cost_estimate=pl.CostEstimate(
            flops=6 * rows * units * model, bytes_accessed=6 * units * model, transcendentals=rows * units
        ),
        name="experts",
    )(place, near, far, *params, *weights)


def shift(x, axis, by):
    size = lax.axis_size(axis)
    return lax.ppermute(x, axis, [(i, (i + by) % size) for i in range(size)])


def add(*terms):
    return sum(t.astype(jnp.float32) for t in terms)


def per_device(
    queries, new_kv, kv_cache, cache_len, residual, norm_gain, router, routes, gate_w, up_w, down_w
):
    groups, tensors = lax.axis_size("group"), lax.axis_size("tensor")
    experts, block = router.shape
    own_params = jnp.concatenate([router, norm_gain[None, :], jnp.zeros((7, block), router.dtype)], axis=0)
    params = [own_params] + [shift(own_params, "tensor", k) for k in range(1, tensors)]
    place = lax.axis_index("tensor")
    where = jnp.stack([place, lax.axis_index("section") * tensors + place]).astype(jnp.int32)

    fresh = attend(cache_len, queries, new_kv, kv_cache, residual, routes)
    rows = jnp.stack([fresh] + [shift(fresh, "tensor", k) for k in range(1, tensors)])
    near = jnp.stack([rows] + [shift(rows, "group", k) for k in range(1, groups)])
    far = shift(near, "section", 1)

    mine, theirs = run_expert(where, near, far, params, gate_w, up_w, down_w, experts)
    both = add(mine, shift(theirs, "section", 1)).astype(jnp.bfloat16)
    got = add(both[0], *[shift(both[k], "group", -k) for k in range(1, groups)]).astype(jnp.bfloat16)
    mixed = add(fresh[:, :block], got[0], *[shift(got[k], "tensor", -k) for k in range(1, tensors)])
    return mixed.astype(jnp.bfloat16)


def solution(mesh):
    rows = P(("section", "group"), "tensor")
    weights = P(("section", "tensor"), "group", None)
    in_specs = (
        rows,
        rows,
        P(("section", "group"), None, "tensor"),
        P(("section", "group")),
        rows,
        P("tensor"),
        P(None, "tensor"),
        P(("section", "group"), None),
        weights,
        weights,
        weights,
    )
    return jax.shard_map(per_device, mesh=mesh, in_specs=in_specs, out_specs=rows, check_vma=False)
```

time: 125 us -> 71.6 us (0.57)
  blocking collectives: 57.4 us -> 0 us
  matrix products: 17.1 us -> 0 us
  starting transfers between devices: 4.61 us -> 19.5 us
  between operations: 14.2 us -> 0.75 us
  Pallas kernels: 0 us -> 11.8 us
  local copies, waits for them, and re-layouts: 12.1 us -> 17.2 us
  waiting for transfers between devices: 16.2 us -> 20.2 us
    all_gather x3 -> x0, blocking collectives: 41 us -> none  [the longest x1 14.7 us: per_device(): lax.all_gather(stream, 'tensor', axis=1, tiled=True)]
    ppermute x0 -> x17, waiting for transfers between devices: none -> 20.2 us  [shift(): return lax.ppermute(x, axis, [(i, (i + by) % size) for i in range(size)])]
    ppermute x0 -> x17, starting transfers between devices: none -> 19.5 us  [shift(): return lax.ppermute(x, axis, [(i, (i + by) % size) for i in range(size)])]
    dot_general x9 -> x0, matrix products: 17.1 us -> none  [the longest x1 7.47 us: per_device(): lax.dot_general(flat_rows, gate_local, (((1,), (1,)), ((), ())), preferre...]
    all_to_all x2 -> x0, blocking collectives: 16.4 us -> none  [the longest x1 11.7 us: per_device(): lax.all_to_all(spread_rows, ('section', 'group'), split_axis=0, concat_ax...]
    pallas_call x0 -> x2, Pallas kernels: none -> 11.8 us  [the longest x1 10.4 us: run_expert(): pl.pallas_call(functools.partial(expert_kernel, ranks=ranks, tensors=tens...]
    reduce_scatter x1 -> x0, waiting for transfers between devices: 10.5 us -> none  [per_device(): lax.psum_scatter(jnp.dot(hidden, down_local, preferred_element_type=jnp.f...]
    unnamed x17 -> x16, local copies, waits for them, and re-layouts: 8.66 us -> 16.4 us
  transfers between devices with their start and end apart: 2 -> 17, of which waited for: 2 -> 13; matrix products, arithmetic and copies ran while one was open for 0% -> 2% of each run, Pallas kernels for 0% -> 0%
where the time goes in v1:
time: 71.6 us; the launch traced here: 71.1 us
  waiting for transfers between devices  20.2 us (28%)
  starting transfers between devices  19.5 us (27%)
  local copies, waits for them, and re-layouts  17.2 us (24%)
  Pallas kernels  11.8 us (16%)
  other arithmetic  1.6 us (2%)
  between operations  0.75 us (1%)
    ppermute x17, waiting for transfers between devices, shift(): return lax.ppermute(x, axis, [(i, (i + by) % size) for i in range(size)])  20.2 us
    ppermute x17, starting transfers between devices, shift(): return lax.ppermute(x, axis, [(i, (i + by) % size) for i in range(size)])  19.5 us
    unnamed x16, local copies, waits for them, and re-layouts  16.4 us
    pallas_call x1, Pallas kernels, run_expert(): pl.pallas_call(functools.partial(expert_kernel, ranks=ranks, tensors=tens...  10.4 us
  transfers between devices with their start and end apart: 17, of which 13 were waited for; matrix products, arithmetic and copies ran while one was open for 2% of the time, Pallas kernels for 0%

profile of v1, /device:TPU:0, one launch (start us, length us, event | category | flops | bytes accessed | tf_op | source)
XLA Modules:
  0.0 71.1 jit_solution(13454831199908392123)
XLA Ops:
  0.7 1.6 %copy-done.3 = bf16[1,2048,512]{2,1,0:T(8,128)(2,1)S(1)} copy-done((bf16[1,2048,512]{2,1,0:T(8,128)(2,1)S(1)}, bf16[1,2048,512]{2,1,0:T(8,128)(2,1)}, u32[]{:S(2)}) %copy-start.3) | copy-done | bytes 2097176
  2.2 0.7 copy-done.4
  3.0 0.7 copy-done.5
  3.7 0.7 copy-done.6
  4.4 0.7 copy-done.7
  5.0 1.4 %attention.1 = bf16[8,896]{1,0:T(8,128)(2,1)S(1)} custom-call(s32[1]{0:T(128)S(6)} %copy.12.len_ref, bf16[8,768]{1,0:T(8,128)(2,1)S(1)} %copy-done.4, bf16[8,512]{1,0:T(8,128)(2,1)S(1)} %copy-done.6, bf16[1,2048,512]{2,1,0:T(8,128)(2,1)S(1)} %copy-done.3, bf16[8,768]{1,0:T(8,128)(2,1)S(1)} %copy-done.5, s32[4,8]{1,0:T(4,128)S(1)} %bitcast.35), custom_call_target="tpu_custom_call" | custom-call | flops 50331648 | bytes 2097152 | tf_op jit(solution)/shard_map/attention/pallas_call | solution.py:83
  6.4 5.1 %collective-permute-start.2 = (bf16[8,896]{1,0:T(8,128)(2,1)S(1)}, bf16[8,896]{1,0:T(8,128)(2,1)S(1)}, u32[]{:S(2)}, u32[]{:S(2)}) collective-permute-start(bf16[8,896]{1,0:T(8,128)(2,1)S(1)} %attention.1), channel_id=1, source_target_pairs={{0,3},{1,0},{2,1},{3,2},{4,7},{5,4},{6,5},{7,6},{8,11},{9,8},{10,9... | collective-permute-start | bytes 43016 | tf_op jit(solution)/shard_map/ppermute | solution.py:207
  11.5 1.0 %collective-permute-start = (bf16[8,896]{1,0:T(8,128)(2,1)S(1)}, bf16[8,896]{1,0:T(8,128)(2,1)S(1)}, u32[]{:S(2)}, u32[]{:S(2)}) collective-permute-start(bf16[8,896]{1,0:T(8,128)(2,1)S(1)} %attention.1), channel_id=1, source_target_pairs={{0,1},{1,2},{2,3},{3,0},{4,5},{5,6},{6,7},{7,4},{8,9},{9,10},{10,1... | collective-permute-start | bytes 43016 | tf_op jit(solution)/shard_map/ppermute | solution.py:207
  13.0 3.2 %collective-permute-done.1 = bf16[8,896]{1,0:T(8,128)(2,1)S(1)} collective-permute-done((bf16[8,896]{1,0:T(8,128)(2,1)S(1)}, bf16[8,896]{1,0:T(8,128)(2,1)S(1)}, u32[]{:S(2)}, u32[]{:S(2)}) %collective-permute-start.1) | collective-permute-done | bytes 14368 | tf_op jit(solution)/shard_map/ppermute | solution.py:207
  16.1 0.9 %collective-permute-done = bf16[8,896]{1,0:T(8,128)(2,1)S(1)} collective-permute-done((bf16[8,896]{1,0:T(8,128)(2,1)S(1)}, bf16[8,896]{1,0:T(8,128)(2,1)S(1)}, u32[]{:S(2)}, u32[]{:S(2)}) %collective-permute-start) | collective-permute-done | bytes 14368 | tf_op jit(solution)/shard_map/ppermute | solution.py:207
  17.1 1.6 %collective-permute-start.4 = (bf16[4,8,896]{2,1,0:T(8,128)(2,1)S(1)}, bf16[4,8,896]{2,1,0:T(8,128)(2,1)S(1)}, u32[]{:S(2)}, u32[]{:S(2)}) collective-permute-start(bf16[4,8,896]{2,1,0:T(8,128)(2,1)S(1)} %get-tuple-element.13), channel_id=1, source_target_pairs={{0,8},{4,12},{8,0},{12,4},{1,9},{5,13},{9,1},{13,5},{2,10},{6,14},... | collective-permute-start | bytes 172040 | tf_op jit(solution)/shard_map/ppermute | solution.py:207
  18.7 1.5 %collective-permute-start.3 = (bf16[4,8,896]{2,1,0:T(8,128)(2,1)S(1)}, bf16[4,8,896]{2,1,0:T(8,128)(2,1)S(1)}, u32[]{:S(2)}, u32[]{:S(2)}) collective-permute-start(bf16[4,8,896]{2,1,0:T(8,128)(2,1)S(1)} %get-tuple-element.13), channel_id=1, source_target_pairs={{0,4},{4,8},{8,12},{12,0},{1,5},{5,9},{9,13},{13,1},{2,6},{6,10},{... | collective-permute-start | bytes 172040 | tf_op jit(solution)/shard_map/ppermute | solution.py:207
  20.1 1.4 %collective-permute-start.5 = (bf16[4,8,896]{2,1,0:T(8,128)(2,1)S(1)}, bf16[4,8,896]{2,1,0:T(8,128)(2,1)S(1)}, u32[]{:S(2)}, u32[]{:S(2)}) collective-permute-start(bf16[4,8,896]{2,1,0:T(8,128)(2,1)S(1)} %get-tuple-element.13), channel_id=1, source_target_pairs={{0,12},{4,0},{8,4},{12,8},{1,13},{5,1},{9,5},{13,9},{2,14},{6,2},{... | collective-permute-start | bytes 172040 | tf_op jit(solution)/shard_map/ppermute | solution.py:207
  21.6 0.7 broadcast_in_dim.6
  22.4 1.4 %collective-permute-done.3 = bf16[4,8,896]{2,1,0:T(8,128)(2,1)S(1)} collective-permute-done((bf16[4,8,896]{2,1,0:T(8,128)(2,1)S(1)}, bf16[4,8,896]{2,1,0:T(8,128)(2,1)S(1)}, u32[]{:S(2)}, u32[]{:S(2)}) %collective-permute-start.3) | collective-permute-done | bytes 57376 | tf_op jit(solution)/shard_map/ppermute | solution.py:207
  24.4 0.8 %maximum_maximum_fusion.refs_0_ = bf16[16,768]{1,0:T(8,128)(2,1)S(1)} fusion(bf16[1,768]{1,0:T(2,128)(2,1)S(1)} %broadcast_in_dim.6, bf16[8,768]{1,0:T(8,128)(2,1)} %param.17, bf16[16]{0:T(256)(128)(2,1)S(1)} %pad.2.clone), kind=kLoop, calls=%fused_computation.11 | loop fusion | flops 73728 | bytes 38432 | tf_op jit(solution)/shard_map/concatenate | solution.py:219
  25.8 0.6 collective-permute-start.8
  26.4 2.0 %collective-permute-start.7 = (bf16[16,768]{1,0:T(8,128)(2,1)S(1)}, bf16[16,768]{1,0:T(8,128)(2,1)S(1)}, u32[]{:S(2)}, u32[]{:S(2)}) collective-permute-start(bf16[16,768]{1,0:T(8,128)(2,1)S(1)} %maximum_maximum_fusion.refs_0_), channel_id=1, source_target_pairs={{0,1},{1,2},{2,3},{3,0},{4,5},{5,6},{6,7},{7,4},{8,9},{9,10},{10,1... | collective-permute-start | bytes 73736 | tf_op jit(solution)/shard_map/ppermute | solution.py:207
  29.1 1.7 %collective-permute-done.8.refs_2_ = bf16[16,768]{1,0:T(8,128)(2,1)S(1)} collective-permute-done((bf16[16,768]{1,0:T(8,128)(2,1)S(1)}, bf16[16,768]{1,0:T(8,128)(2,1)S(1)}, u32[]{:S(2)}, u32[]{:S(2)}) %collective-permute-start.8) | collective-permute-done | bytes 24608 | tf_op jit(solution)/shard_map/ppermute | solution.py:207
  30.8 1.3 %collective-permute-done.7.refs_1_ = bf16[16,768]{1,0:T(8,128)(2,1)S(1)} collective-permute-done((bf16[16,768]{1,0:T(8,128)(2,1)S(1)}, bf16[16,768]{1,0:T(8,128)(2,1)S(1)}, u32[]{:S(2)}, u32[]{:S(2)}) %collective-permute-start.7) | collective-permute-done | bytes 24608 | tf_op jit(solution)/shard_map/ppermute | solution.py:207
  32.1 4.0 %copy-done = bf16[1,1728,3072]{2,1,0:T(8,128)(2,1)S(1)} copy-done((bf16[1,1728,3072]{2,1,0:T(8,128)(2,1)S(1)}, bf16[1,1728,3072]{2,1,0:T(8,128)(2,1)}, u32[]{:S(2)}) %copy-start) | copy-done | bytes 10616856
  36.1 4.0 %copy-done.1 = bf16[1,1728,3072]{2,1,0:T(8,128)(2,1)S(1)} copy-done((bf16[1,1728,3072]{2,1,0:T(8,128)(2,1)S(1)}, bf16[1,1728,3072]{2,1,0:T(8,128)(2,1)}, u32[]{:S(2)}) %copy-start.1) | copy-done | bytes 10616856
  40.1 4.0 %copy-done.2 = bf16[1,1728,3072]{2,1,0:T(8,128)(2,1)S(1)} copy-done((bf16[1,1728,3072]{2,1,0:T(8,128)(2,1)S(1)}, bf16[1,1728,3072]{2,1,0:T(8,128)(2,1)}, u32[]{:S(2)}) %copy-start.2) | copy-done | bytes 10616856
  44.1 10.4 %experts.1 = (bf16[4,4,8,768]{3,2,1,0:T(8,128)(2,1)S(1)}, bf16[4,4,8,768]{3,2,1,0:T(8,128)(2,1)S(1)}) custom-call(s32[2]{0:T(128)S(1)} %pad_add_fusion.place_ref, bf16[4,4,8,896]{3,2,1,0:T(8,128)(2,1)S(1)} %pad_maximum_fusion.near_ref, bf16[4,4,8,896]{3,2,1,0:T(8,128)(2,1)S(1)} %collective-permute-done.6.far_ref, ...), custom_call_target="tpu_custom_call" | custom-call | flops 2038431744 | bytes 31850496 | tf_op jit(solution)/shard_map/experts/pallas_call | solution.py:187
  54.6 1.4 %collective-permute-done.10 = bf16[4,4,8,768]{3,2,1,0:T(8,128)(2,1)S(1)} collective-permute-done((bf16[4,4,8,768]{3,2,1,0:T(8,128)(2,1)S(1)}, bf16[4,4,8,768]{3,2,1,0:T(8,128)(2,1)S(1)}, u32[]{:S(2)}, u32[]{:S(2)}) %collective-permute-start.10) | collective-permute-done | bytes 196640 | tf_op jit(solution)/shard_map/ppermute | solution.py:207
  56.1 2.4 %collective-permute-start.11 = (bf16[4,8,768]{2,1,0:T(8,128)(2,1)S(1)}, bf16[4,8,768]{2,1,0:T(8,128)(2,1)S(1)}, u32[]{:S(2)}, u32[]{:S(2)}) collective-permute-start(bf16[4,8,768]{2,1,0:T(8,128)(2,1)S(1)} %get-tuple-element.9), channel_id=1, source_target_pairs={{0,12},{4,0},{8,4},{12,8},{1,13},{5,1},{9,5},{13,9},{2,14},{6,2},{... | collective-permute-start | bytes 147464 | tf_op jit(solution)/shard_map/ppermute | solution.py:207
  59.1 1.2 %collective-permute-done.11 = bf16[4,8,768]{2,1,0:T(8,128)(2,1)S(1)} collective-permute-done((bf16[4,8,768]{2,1,0:T(8,128)(2,1)S(1)}, bf16[4,8,768]{2,1,0:T(8,128)(2,1)S(1)}, u32[]{:S(2)}, u32[]{:S(2)}) %collective-permute-start.11) | collective-permute-done | bytes 49184 | tf_op jit(solution)/shard_map/ppermute | solution.py:207
  60.3 3.2 %collective-permute-done.13 = bf16[4,8,768]{2,1,0:T(8,128)(2,1)S(1)} collective-permute-done((bf16[4,8,768]{2,1,0:T(8,128)(2,1)S(1)}, bf16[4,8,768]{2,1,0:T(8,128)(2,1)S(1)}, u32[]{:S(2)}, u32[]{:S(2)}) %collective-permute-start.13) | collective-permute-done | bytes 49184 | tf_op jit(solution)/shard_map/ppermute | solution.py:207
  63.5 1.4 %collective-permute-start.14 = (bf16[8,768]{1,0:T(8,128)(2,1)S(1)}, bf16[8,768]{1,0:T(8,128)(2,1)S(1)}, u32[]{:S(2)}, u32[]{:S(2)}) collective-permute-start(bf16[8,768]{1,0:T(8,128)(2,1)S(1)} %get-tuple-element.14), channel_id=1, source_target_pairs={{0,3},{1,0},{2,1},{3,2},{4,7},{5,4},{6,5},{7,6},{8,11},{9,8},{10,9... | collective-permute-start | bytes 36872 | tf_op jit(solution)/shard_map/ppermute | solution.py:207
  65.0 0.6 collective-permute-start.16
  66.1 1.2 %collective-permute-done.14 = bf16[8,768]{1,0:T(8,128)(2,1)S(1)} collective-permute-done((bf16[8,768]{1,0:T(8,128)(2,1)S(1)}, bf16[8,768]{1,0:T(8,128)(2,1)S(1)}, u32[]{:S(2)}, u32[]{:S(2)}) %collective-permute-start.14) | collective-permute-done | bytes 12320 | tf_op jit(solution)/shard_map/ppermute | solution.py:207
  67.3 3.2 %collective-permute-done.16 = bf16[8,768]{1,0:T(8,128)(2,1)S(1)} collective-permute-done((bf16[8,768]{1,0:T(8,128)(2,1)S(1)}, bf16[8,768]{1,0:T(8,128)(2,1)S(1)}, u32[]{:S(2)}, u32[]{:S(2)}) %collective-permute-start.16) | collective-permute-done | bytes 12320 | tf_op jit(solution)/shard_map/ppermute | solution.py:207
  (32 shorter events, 4.4 us)
Async XLA Ops:
  0.7 1.6 %copy-start.3 = (bf16[1,2048,512]{2,1,0:T(8,128)(2,1)S(1)}, bf16[1,2048,512]{2,1,0:T(8,128)(2,1)}, u32[]{:S(2)}) copy-start(bf16[1,2048,512]{2,1,0:T(8,128)(2,1)} %kv_hbm.1) | copy-start | bytes 6291460
  2.2 0.7 copy-start.4
  3.0 0.7 copy-start.5
  3.7 0.7 copy-start.6
  4.4 0.7 copy-start.7
  6.4 6.5 %collective-permute-start.2 = (bf16[8,896]{1,0:T(8,128)(2,1)S(1)}, bf16[8,896]{1,0:T(8,128)(2,1)S(1)}, u32[]{:S(2)}, u32[]{:S(2)}) collective-permute-start(bf16[8,896]{1,0:T(8,128)(2,1)S(1)} %attention.1), channel_id=1, source_target_pairs={{0,3},{1,0},{2,1},{3,2},{4,7},{5,4},{6,5},{7,6},{8,11},{9,8},{10,9... | collective-permute-start | bytes 43016 | tf_op jit(solution)/shard_map/ppermute | solution.py:207
  11.5 4.6 %collective-permute-start.1 = (bf16[8,896]{1,0:T(8,128)(2,1)S(1)}, bf16[8,896]{1,0:T(8,128)(2,1)S(1)}, u32[]{:S(2)}, u32[]{:S(2)}) collective-permute-start(bf16[8,896]{1,0:T(8,128)(2,1)S(1)} %attention.1), channel_id=1, source_target_pairs={{0,2},{1,3},{2,0},{3,1},{4,6},{5,7},{6,4},{7,5},{8,10},{9,11},{10,... | collective-permute-start | bytes 43016 | tf_op jit(solution)/shard_map/ppermute | solution.py:207
  11.5 5.5 %collective-permute-start = (bf16[8,896]{1,0:T(8,128)(2,1)S(1)}, bf16[8,896]{1,0:T(8,128)(2,1)S(1)}, u32[]{:S(2)}, u32[]{:S(2)}) collective-permute-start(bf16[8,896]{1,0:T(8,128)(2,1)S(1)} %attention.1), channel_id=1, source_target_pairs={{0,1},{1,2},{2,3},{3,0},{4,5},{5,6},{6,7},{7,4},{8,9},{9,10},{10,1... | collective-permute-start | bytes 43016 | tf_op jit(solution)/shard_map/ppermute | solution.py:207
  17.1 5.3 %collective-permute-start.4 = (bf16[4,8,896]{2,1,0:T(8,128)(2,1)S(1)}, bf16[4,8,896]{2,1,0:T(8,128)(2,1)S(1)}, u32[]{:S(2)}, u32[]{:S(2)}) collective-permute-start(bf16[4,8,896]{2,1,0:T(8,128)(2,1)S(1)} %get-tuple-element.13), channel_id=1, source_target_pairs={{0,8},{4,12},{8,0},{12,4},{1,9},{5,13},{9,1},{13,5},{2,10},{6,14},... | collective-permute-start | bytes 172040 | tf_op jit(solution)/shard_map/ppermute | solution.py:207
  18.7 5.1 %collective-permute-start.3 = (bf16[4,8,896]{2,1,0:T(8,128)(2,1)S(1)}, bf16[4,8,896]{2,1,0:T(8,128)(2,1)S(1)}, u32[]{:S(2)}, u32[]{:S(2)}) collective-permute-start(bf16[4,8,896]{2,1,0:T(8,128)(2,1)S(1)} %get-tuple-element.13), channel_id=1, source_target_pairs={{0,4},{4,8},{8,12},{12,0},{1,5},{5,9},{9,13},{13,1},{2,6},{6,10},{... | collective-permute-start | bytes 172040 | tf_op jit(solution)/shard_map/ppermute | solution.py:207
  20.1 4.2 %collective-permute-start.5 = (bf16[4,8,896]{2,1,0:T(8,128)(2,1)S(1)}, bf16[4,8,896]{2,1,0:T(8,128)(2,1)S(1)}, u32[]{:S(2)}, u32[]{:S(2)}) collective-permute-start(bf16[4,8,896]{2,1,0:T(8,128)(2,1)S(1)} %get-tuple-element.13), channel_id=1, source_target_pairs={{0,12},{4,0},{8,4},{12,8},{1,13},{5,1},{9,5},{13,9},{2,14},{6,2},{... | collective-permute-start | bytes 172040 | tf_op jit(solution)/shard_map/ppermute | solution.py:207
  24.4 7.7 %collective-permute-start.6 = (bf16[4,4,8,896]{3,2,1,0:T(8,128)(2,1)S(1)}, bf16[4,4,8,896]{3,2,1,0:T(8,128)(2,1)S(1)}, u32[]{:S(2)}, u32[]{:S(2)}) collective-permute-start(bf16[4,4,8,896]{3,2,1,0:T(8,128)(2,1)S(1)} %pad_maximum_fusion.near_ref), channel_id=1, source_target_pairs={{0,16},{16,0},{1,17},{17,1},{2,18},{18,2},{3,19},{19,3},{4,20},{20... | collective-permute-start | bytes 688136 | tf_op jit(solution)/shard_map/ppermute | solution.py:207
  25.2 3.8 %collective-permute-start.9 = (bf16[16,768]{1,0:T(8,128)(2,1)S(1)}, bf16[16,768]{1,0:T(8,128)(2,1)S(1)}, u32[]{:S(2)}, u32[]{:S(2)}) collective-permute-start(bf16[16,768]{1,0:T(8,128)(2,1)S(1)} %maximum_maximum_fusion.refs_0_), channel_id=1, source_target_pairs={{0,3},{1,0},{2,1},{3,2},{4,7},{5,4},{6,5},{7,6},{8,11},{9,8},{10,9... | collective-permute-start | bytes 73736 | tf_op jit(solution)/shard_map/ppermute | solution.py:207
  25.8 5.0 %collective-permute-start.8 = (bf16[16,768]{1,0:T(8,128)(2,1)S(1)}, bf16[16,768]{1,0:T(8,128)(2,1)S(1)}, u32[]{:S(2)}, u32[]{:S(2)}) collective-permute-start(bf16[16,768]{1,0:T(8,128)(2,1)S(1)} %maximum_maximum_fusion.refs_0_), channel_id=1, source_target_pairs={{0,2},{1,3},{2,0},{3,1},{4,6},{5,7},{6,4},{7,5},{8,10},{9,11},{10,... | collective-permute-start | bytes 73736 | tf_op jit(solution)/shard_map/ppermute | solution.py:207
  26.4 5.6 %collective-permute-start.7 = (bf16[16,768]{1,0:T(8,128)(2,1)S(1)}, bf16[16,768]{1,0:T(8,128)(2,1)S(1)}, u32[]{:S(2)}, u32[]{:S(2)}) collective-permute-start(bf16[16,768]{1,0:T(8,128)(2,1)S(1)} %maximum_maximum_fusion.refs_0_), channel_id=1, source_target_pairs={{0,1},{1,2},{2,3},{3,0},{4,5},{5,6},{6,7},{7,4},{8,9},{9,10},{10,1... | collective-permute-start | bytes 73736 | tf_op jit(solution)/shard_map/ppermute | solution.py:207
  32.1 4.0 %copy-start = (bf16[1,1728,3072]{2,1,0:T(8,128)(2,1)S(1)}, bf16[1,1728,3072]{2,1,0:T(8,128)(2,1)}, u32[]{:S(2)}) copy-start(bf16[1,1728,3072]{2,1,0:T(8,128)(2,1)} %refs_4_.1) | copy-start | bytes 31850500
  36.1 4.0 %copy-start.1 = (bf16[1,1728,3072]{2,1,0:T(8,128)(2,1)S(1)}, bf16[1,1728,3072]{2,1,0:T(8,128)(2,1)}, u32[]{:S(2)}) copy-start(bf16[1,1728,3072]{2,1,0:T(8,128)(2,1)} %refs_5_.1) | copy-start | bytes 31850500
  40.1 4.0 %copy-start.2 = (bf16[1,1728,3072]{2,1,0:T(8,128)(2,1)S(1)}, bf16[1,1728,3072]{2,1,0:T(8,128)(2,1)}, u32[]{:S(2)}) copy-start(bf16[1,1728,3072]{2,1,0:T(8,128)(2,1)} %refs_6_.1) | copy-start | bytes 31850500
  54.5 1.5 %collective-permute-start.10 = (bf16[4,4,8,768]{3,2,1,0:T(8,128)(2,1)S(1)}, bf16[4,4,8,768]{3,2,1,0:T(8,128)(2,1)S(1)}, u32[]{:S(2)}, u32[]{:S(2)}) collective-permute-start(bf16[4,4,8,768]{3,2,1,0:T(8,128)(2,1)S(1)} %get-tuple-element.8), channel_id=1, source_target_pairs={{0,16},{16,0},{1,17},{17,1},{2,18},{18,2},{3,19},{19,3},{4,20},{20... | collective-permute-start | bytes 589832 | tf_op jit(solution)/shard_map/ppermute | solution.py:207
  56.1 4.2 %collective-permute-start.11 = (bf16[4,8,768]{2,1,0:T(8,128)(2,1)S(1)}, bf16[4,8,768]{2,1,0:T(8,128)(2,1)S(1)}, u32[]{:S(2)}, u32[]{:S(2)}) collective-permute-start(bf16[4,8,768]{2,1,0:T(8,128)(2,1)S(1)} %get-tuple-element.9), channel_id=1, source_target_pairs={{0,12},{4,0},{8,4},{12,8},{1,13},{5,1},{9,5},{13,9},{2,14},{6,2},{... | collective-permute-start | bytes 147464 | tf_op jit(solution)/shard_map/ppermute | solution.py:207
  58.5 5.0 %collective-permute-start.13 = (bf16[4,8,768]{2,1,0:T(8,128)(2,1)S(1)}, bf16[4,8,768]{2,1,0:T(8,128)(2,1)S(1)}, u32[]{:S(2)}, u32[]{:S(2)}) collective-permute-start(bf16[4,8,768]{2,1,0:T(8,128)(2,1)S(1)} %get-tuple-element.10), channel_id=1, source_target_pairs={{0,4},{4,8},{8,12},{12,0},{1,5},{5,9},{9,13},{13,1},{2,6},{6,10},{... | collective-permute-start | bytes 147464 | tf_op jit(solution)/shard_map/ppermute | solution.py:207
  58.5 5.0 %collective-permute-start.12 = (bf16[4,8,768]{2,1,0:T(8,128)(2,1)S(1)}, bf16[4,8,768]{2,1,0:T(8,128)(2,1)S(1)}, u32[]{:S(2)}, u32[]{:S(2)}) collective-permute-start(bf16[4,8,768]{2,1,0:T(8,128)(2,1)S(1)} %get-tuple-element.11), channel_id=1, source_target_pairs={{0,8},{4,12},{8,0},{12,4},{1,9},{5,13},{9,1},{13,5},{2,10},{6,14},... | collective-permute-start | bytes 147464 | tf_op jit(solution)/shard_map/ppermute | solution.py:207
  63.5 3.7 %collective-permute-start.14 = (bf16[8,768]{1,0:T(8,128)(2,1)S(1)}, bf16[8,768]{1,0:T(8,128)(2,1)S(1)}, u32[]{:S(2)}, u32[]{:S(2)}) collective-permute-start(bf16[8,768]{1,0:T(8,128)(2,1)S(1)} %get-tuple-element.14), channel_id=1, source_target_pairs={{0,3},{1,0},{2,1},{3,2},{4,7},{5,4},{6,5},{7,6},{8,11},{9,8},{10,9... | collective-permute-start | bytes 36872 | tf_op jit(solution)/shard_map/ppermute | solution.py:207
  65.0 5.5 %collective-permute-start.16 = (bf16[8,768]{1,0:T(8,128)(2,1)S(1)}, bf16[8,768]{1,0:T(8,128)(2,1)S(1)}, u32[]{:S(2)}, u32[]{:S(2)}) collective-permute-start(bf16[8,768]{1,0:T(8,128)(2,1)S(1)} %get-tuple-element.15), channel_id=1, source_target_pairs={{0,1},{1,2},{2,3},{3,0},{4,5},{5,6},{6,7},{7,4},{8,9},{9,10},{10,1... | collective-permute-start | bytes 36872 | tf_op jit(solution)/shard_map/ppermute | solution.py:207
  65.6 4.9 %collective-permute-start.15 = (bf16[8,768]{1,0:T(8,128)(2,1)S(1)}, bf16[8,768]{1,0:T(8,128)(2,1)S(1)}, u32[]{:S(2)}, u32[]{:S(2)}) collective-permute-start(bf16[8,768]{1,0:T(8,128)(2,1)S(1)} %get-tuple-element.16), channel_id=1, source_target_pairs={{0,2},{1,3},{2,0},{3,1},{4,6},{5,7},{6,4},{7,5},{8,10},{9,11},{10,... | collective-permute-start | bytes 36872 | tf_op jit(solution)/shard_map/ppermute | solution.py:207
